TPU v7x, 32 devices: a whole 2x2x4 slice. The times are simulated.
32 devices in a mesh: gx: 8 (over z, y), gy: 4 (over x, core).
Axes of the slice: x: 2, y: 2, z: 4, core: 2. Of those that a mesh axis runs over, the one named last changes fastest.
Arguments:
- latent: bfloat16 [32, 512, 128], P('gx', 'gy'), may hold values from -6 to 6
- corr_kernel: bfloat16 [32, 128], replicated, may hold values from -1 to 1
- first_conv_weight: bfloat16 [3, 3, 128, 128], replicated, may hold values from -0.1875 to 0.1875
- first_conv_bias: float32 [128], replicated, may hold values from -3 to 3
- second_conv_weight: bfloat16 [3, 3, 128, 128], replicated, may hold values from -0.1875 to 0.1875
- second_conv_bias: float32 [128], replicated, may hold values from -3 to 3
- cotangent: bfloat16 [32, 512, 128], P('gx', 'gy'), may hold values from -0.046875 to 0.046875
Outputs:
- prediction: bfloat16 [32, 512, 128], P('gx', 'gy')
- conv1_weight_grad: float32 [3, 3, 128, 128], replicated
- conv1_bias_grad: float32 [128], replicated
- conv2_weight_grad: float32 [3, 3, 128, 128], replicated
- conv2_bias_grad: float32 [128], replicated
- kernel_grad: float32 [32, 128], replicated
All inputs are finite; a program needn't handle non-finite values.
Results may differ from a plain program's by a relative error of at most 0.0095.
Values may be sent and summed in bfloat16 or wider, within the bound.
A program may use at most 64 MiB of HBM per device.

v0:
```python
import math

import jax
import jax.numpy as jnp
from jax import lax
from jax.sharding import PartitionSpec as P

DILATION_FIRST = 1
DILATION_SECOND = 2


def padded_2(array, sides, width):
    for axis, dim in sides:
        size, length = (lax.axis_size(axis), array.shape[dim])
        up = [(i, (i + 1) % size) for i in range(size)]
        down = [(j, i) for i, j in up]
        last = lax.slice_in_dim(array, length - width, length, axis=dim)
        leading = lax.slice_in_dim(array, 0, width, axis=dim)
        before = lax.ppermute(last, axis, up)
        after = lax.ppermute(leading, axis, down)
        array = jnp.concatenate([before, array, after], axis=dim)
    return array


def silu_slope(preact):
    logistic = jax.nn.sigmoid(preact)
    return logistic * (1.0 + preact * (1.0 - logistic))


def spectral_tables(length):
    positions = jnp.arange(length, dtype=jnp.int32)
    phases = positions[:, None] * positions[None, :] % length
    angles = phases.astype(jnp.float32) * (2.0 * math.pi / length)
    return (jnp.cos(angles), jnp.sin(angles))


def transform(table_mat, operand):
    return jnp.dot(
        table_mat, operand, precision=lax.Precision.HIGHEST, preferred_element_type=jnp.float32
    )


def to_columns(field):
    return lax.all_to_all(field, "gx", split_axis=1, concat_axis=0, tiled=True)


def surround(field, dilation):
    return padded_2(field, (("gx", 0), ("gy", 1)), dilation)


def forward_taps(padded, dilation, row_count, col_count, channels):
    windows = []
    for row_off in (-1, 0, 1):
        for col_off in (-1, 0, 1):
            row_at = dilation + row_off * dilation
            col_at = dilation + col_off * dilation
            windows.append(padded[row_at : row_at + row_count, col_at : col_at + col_count])
    return jnp.concatenate(windows, axis=-1).reshape(-1, 9 * channels)


def backward_taps(padded, dilation, row_count, col_count, channels):
    windows = []
    for row_off in (-1, 0, 1):
        for col_off in (-1, 0, 1):
            row_at = dilation - row_off * dilation
            col_at = dilation - col_off * dilation
            windows.append(padded[row_at : row_at + row_count, col_at : col_at + col_count])
    return jnp.concatenate(windows, axis=-1).reshape(-1, 9 * channels)


def layer_back(stored_item, gradient, row_count, col_count, channels):
    stacked, preact, weight, dilation = stored_item
    slope = (gradient * silu_slope(preact)).astype(jnp.bfloat16)
    flat_slope = slope.reshape(-1, channels)
    weight_grad = lax.dot_general(
        stacked, flat_slope, (((0,), (0,)), ((), ())), preferred_element_type=jnp.float32
    ).reshape(3, 3, channels, channels)
    bias_grad = jnp.sum(flat_slope.astype(jnp.float32), axis=0)
    stacked_back = backward_taps(
        surround(slope, dilation), dilation, row_count, col_count, channels
    )
    flipped = jnp.transpose(weight, (0, 1, 3, 2)).reshape(9 * channels, channels)
    carried = gradient + jnp.dot(stacked_back, flipped, preferred_element_type=jnp.float32).reshape(
        gradient.shape
    )
    return (weight_grad, bias_grad, carried)


def per_device(
    latent,
    corr_kernel,
    first_conv_weight,
    first_conv_bias,
    second_conv_weight,
    second_conv_bias,
    cotangent,
):
    row_count, col_count, channels = latent.shape
    full_rows = row_count * lax.axis_size("gx")
    columns = to_columns(latent)
    col_shape = columns.shape
    cosines, sines = spectral_tables(full_rows)
    flattened = columns.reshape(full_rows, -1).astype(jnp.float32)
    lat_real = transform(cosines, flattened).reshape(col_shape)
    lat_imag = (-transform(sines, flattened)).reshape(col_shape)
    kernel_f = corr_kernel.astype(jnp.float32)
    ker_real = transform(cosines, kernel_f)[:, None, :]
    ker_imag = (-transform(sines, kernel_f))[:, None, :]
    prod_real = (lat_real * ker_real + lat_imag * ker_imag).reshape(full_rows, -1)
    prod_imag = (lat_imag * ker_real - lat_real * ker_imag).reshape(full_rows, -1)
    correlated = (transform(cosines, prod_real) - transform(sines, prod_imag)) / full_rows
    mixed_cols = (columns.astype(jnp.float32) + correlated.reshape(col_shape)).astype(jnp.bfloat16)
    mixed_field = lax.all_to_all(mixed_cols, "gx", split_axis=0, concat_axis=1, tiled=True)
    stored = []
    current = mixed_field
    for weight, bias_vec, dilation in (
        (first_conv_weight, first_conv_bias, DILATION_FIRST),
        (second_conv_weight, second_conv_bias, DILATION_SECOND),
    ):
        stacked = forward_taps(
            surround(current, dilation), dilation, row_count, col_count, channels
        )
        preact = (
            jnp.dot(
                stacked, weight.reshape(9 * channels, channels), preferred_element_type=jnp.float32
            )
            + bias_vec
        )
        preact = preact.reshape(current.shape)
        stored.append((stacked, preact, weight, dilation))
        current = (current.astype(jnp.float32) + jax.nn.silu(preact)).astype(jnp.bfloat16)
    gradient = cotangent.astype(jnp.float32)
    second_weight_matrix, bias_two, gradient = layer_back(
        stored[1], gradient, row_count, col_count, channels
    )
    first_weight_matrix, bias_one, gradient = layer_back(
        stored[0], gradient, row_count, col_count, channels
    )
    mixed_gradient = gradient.astype(jnp.bfloat16)
    grad_cols = to_columns(mixed_gradient).reshape(full_rows, -1).astype(jnp.float32)
    grad_real = transform(cosines, grad_cols).reshape(col_shape)
    grad_imag = (-transform(sines, grad_cols)).reshape(col_shape)
    cross_real = jnp.sum(grad_real * lat_real + grad_imag * lat_imag, axis=1)
    cross_imag = jnp.sum(grad_real * lat_imag - grad_imag * lat_real, axis=1)
    kernel_grad = (transform(cosines, cross_real) - transform(sines, cross_imag)) / full_rows
    second_weight_matrix, bias_two, first_weight_matrix, bias_one, kernel_grad = lax.psum(
        (second_weight_matrix, bias_two, first_weight_matrix, bias_one, kernel_grad), ("gx", "gy")
    )
    return (current, first_weight_matrix, bias_one, second_weight_matrix, bias_two, kernel_grad)


def solution(mesh):
    in_specs = (P("gx", "gy", None), P(), P(), P(), P(), P(), P("gx", "gy", None))
    out_specs = (P("gx", "gy", None), P(), P(), P(), P(), P())
    return jax.shard_map(
        per_device, mesh=mesh, in_specs=in_specs, out_specs=out_specs, check_vma=False
    )
```

profile of v0, /device:TPU:1, one launch (start us, length us, event | category | flops | bytes accessed | tf_op | source)
XLA Modules:
  0.0 239.0 jit_solution(1342804127162883692)
XLA Ops:
  7.2 1.7 copy.34
  8.8 6.4 %all-to-all-start = ((bf16[4,128,128]{2,0,1:T(4,128)(2,1)}), bf16[4,128,128]{2,0,1:T(4,128)(2,1)S(1)}, u32[]{:S(2)}, u32[]{:S(2)}) async-start(bf16[4,128,128]{2,0,1:T(4,128)(2,1)} %copy.34), calls=%async_computation | async-start | bytes 262144 | tf_op jit(solution)/shard_map/all_to_all | solution.py:44
  15.2 0.2 convolution_negate_fusion.2
  15.4 0.2 fusion.51
  15.6 5.8 %all-to-all-done = bf16[4,128,128]{2,0,1:T(4,128)(2,1)S(1)} async-done(((bf16[4,128,128]{2,0,1:T(4,128)(2,1)}), bf16[4,128,128]{2,0,1:T(4,128)(2,1)S(1)}, u32[]{:S(2)}, u32[]{:S(2)}) %all-to-all-start) | async-done | bytes 131104 | tf_op jit(solution)/shard_map/all_to_all | solution.py:44
  21.5 0.3 fusion.2
  21.8 0.3 fusion.26
  22.1 0.1 fusion.20
  22.2 0.4 fusion.10
  22.7 0.4 fusion.1
  23.2 8.6 %all_to_all.48 = bf16[32,16,128]{2,1,0:T(8,128)(2,1)S(1)} all-to-all(bf16[32,16,128]{2,1,0:T(8,128)(2,1)S(1)} %fusion.7), channel_id=1, replica_groups=mesh['gx'=8,'gy'=4] {'gx'}, dimensions={0} | all-to-all | bytes 262144 | tf_op jit(solution)/shard_map/all_to_all | solution.py:113
  31.9 4.1 %collective-permute-start.1 = (bf16[1,128,128]{2,1,0:T(8,128)(2,1)S(1)}, bf16[1,128,128]{2,1,0:T(8,128)(2,1)S(1)}, u32[]{:S(2)}, u32[]{:S(2)}) collective-permute-start(bf16[1,128,128]{2,1,0:T(8,128)(2,1)S(1)} %bitcast.201), channel_id=1, source_target_pairs={{4,0},{8,4},{12,8},{16,12},{20,16},{24,20},{28,24},{0,28},{5,1},{9... | collective-permute-start | bytes 98312 | tf_op jit(solution)/shard_map/ppermute | solution.py:20
  36.1 1.3 collective-permute-done
  37.4 5.5 %collective-permute-start.2 = (bf16[6,1,128]{2,1,0:T(2,128)(2,1)S(1)}, bf16[6,1,128]{2,1,0:T(2,128)(2,1)S(1)}, u32[]{:S(2)}, u32[]{:S(2)}) collective-permute-start(bf16[6,1,128]{2,1,0:T(2,128)(2,1)S(1)} %get-tuple-element.41), channel_id=1, source_target_pairs={{0,1},{1,2},{2,3},{3,0},{4,5},{5,6},{6,7},{7,4},{8,9},{9,10},{10,1... | collective-permute-start | bytes 4616 | tf_op jit(solution)/shard_map/ppermute | solution.py:19
  42.9 0.7 collective-permute-done.2
  43.7 2.3 collective-permute-done.3
  45.9 0.1 pad_maximum_fusion.2
  46.0 0.1 fusion.100
  46.5 0.6 copy-done.2
  47.1 0.5 convolution_add_fusion.3
  47.6 0.1 add_convert_fusion.1
  47.8 4.5 %collective-permute-start.5 = (bf16[2,128,128]{2,1,0:T(8,128)(2,1)S(1)}, bf16[2,128,128]{2,1,0:T(8,128)(2,1)S(1)}, u32[]{:S(2)}, u32[]{:S(2)}) collective-permute-start(bf16[2,128,128]{2,1,0:T(8,128)(2,1)S(1)} %get-tuple-element.47), channel_id=1, source_target_pairs={{4,0},{8,4},{12,8},{16,12},{20,16},{24,20},{28,24},{0,28},{5,1},{9... | collective-permute-start | bytes 196616 | tf_op jit(solution)/shard_map/ppermute | solution.py:20
  52.3 1.6 collective-permute-done.4
  53.9 1.6 collective-permute-start.6
  55.5 0.8 collective-permute-done.6
  56.2 2.3 collective-permute-done.7
  58.5 0.1 pad_maximum_fusion
  58.7 0.1 slice_dynamic-update-slice_fusion.16
  58.9 0.1 slice_dynamic-update-slice_fusion.14
  59.1 0.5 copy-done.4
  59.6 1.3 convert_reduce_fusion
  61.0 4.3 %collective-permute-start.9 = (bf16[2,128,128]{2,1,0:T(8,128)(2,1)S(1)}, bf16[2,128,128]{2,1,0:T(8,128)(2,1)S(1)}, u32[]{:S(2)}, u32[]{:S(2)}) collective-permute-start(bf16[2,128,128]{2,1,0:T(8,128)(2,1)S(1)} %get-tuple-element.45), channel_id=1, source_target_pairs={{4,0},{8,4},{12,8},{16,12},{20,16},{24,20},{28,24},{0,28},{5,1},{9... | collective-permute-start | bytes 196616 | tf_op jit(solution)/shard_map/ppermute | solution.py:20
  65.3 1.6 collective-permute-done.8
  66.9 1.7 collective-permute-start.11
  68.7 0.2 copy.43
  68.9 1.1 collective-permute-done.10
  70.0 0.1 maximum_maximum_fusion.1
  70.2 0.1 slice_dynamic-update-slice_fusion.9
  70.4 0.1 slice_dynamic-update-slice_fusion.7
  70.5 1.2 convert_reduce_fusion.1
  71.7 0.6 fusion.102
  72.3 4.3 %collective-permute-start.13 = (bf16[1,128,128]{2,1,0:T(8,128)(2,1)S(1)}, bf16[1,128,128]{2,1,0:T(8,128)(2,1)S(1)}, u32[]{:S(2)}, u32[]{:S(2)}) collective-permute-start(bf16[1,128,128]{2,1,0:T(8,128)(2,1)S(1)} %get-tuple-element.43), channel_id=1, source_target_pairs={{4,0},{8,4},{12,8},{16,12},{20,16},{24,20},{28,24},{0,28},{5,1},{9... | collective-permute-start | bytes 98312 | tf_op jit(solution)/shard_map/ppermute | solution.py:20
  76.6 0.2 copy.45
  76.8 0.6 copy.42
  77.5 1.6 copy.44
  79.1 1.5 collective-permute-start.14
  80.6 0.8 collective-permute-start.15
  81.4 1.3 fusion.108
  82.7 0.1 maximum_maximum_fusion.3
  82.9 0.1 slice_dynamic-update-slice_fusion.3
  83.2 0.5 copy-done.5
  83.7 0.5 fusion.4
  84.2 0.8 copy.46
  84.9 5.2 %all-to-all-start.2 = ((bf16[4,128,128]{2,0,1:T(4,128)(2,1)}), bf16[4,128,128]{2,0,1:T(4,128)(2,1)S(1)}, u32[]{:S(2)}, u32[]{:S(2)}) async-start(bf16[4,128,128]{2,0,1:T(4,128)(2,1)} %copy.46), calls=%async_computation.2 | async-start | bytes 262144 | tf_op jit(solution)/shard_map/all_to_all | solution.py:44
  90.2 1.3 fusion.107
  91.5 4.8 %all-to-all-done.2 = bf16[4,128,128]{2,0,1:T(4,128)(2,1)S(1)} async-done(((bf16[4,128,128]{2,0,1:T(4,128)(2,1)}), bf16[4,128,128]{2,0,1:T(4,128)(2,1)S(1)}, u32[]{:S(2)}, u32[]{:S(2)}) %all-to-all-start.2) | async-done | bytes 131104 | tf_op jit(solution)/shard_map/all_to_all | solution.py:44
  96.3 0.3 fusion.3
  96.7 0.4 fusion.16
  97.1 0.2 fusion.48
  97.3 0.2 fusion.5
  97.5 40.6 %all-reduce = (f32[128]{0:T(128)}, f32[128]{0:T(128)}, f32[32,128]{1,0:T(8,128)}) all-reduce(f32[128]{0:T(128)S(1)} %get-tuple-element.15, f32[128]{0:T(128)S(1)} %get-tuple-element.13, f32[32,128]{1,0:T(8,128)S(1)} %fusion.5), channel_id=1, replica_groups=mesh['gx'=8,'gy'=4] {'gx','gy'}, use_global_device_ids=true, to_apply=%region_2.3 | all-reduce | flops 4352 | bytes 34816 | tf_op jit(solution)/shard_map/psum | solution.py:146
  138.1 91.3 %all-reduce.4.cloned.1.call-done = (f32[3,3,128,128]{3,2,1,0:T(8,128)}, f32[3,3,128,128]{3,2,1,0:T(8,128)}) async-done(((f32[3,3,128,128]{3,2,1,0:T(8,128)}, f32[3,3,128,128]{3,2,1,0:T(8,128)}), (f32[3,3,128,128]{3,2,1,0:T(8,128)}, f32[3,3,128,128]{3,2,1,0:T(8,128)})) %all-reduce.4.cloned.1.call-update) | async-done | bytes 1179664 | tf_op jit(solution)/shard_map/psum | solution.py:146
  229.4 2.0 copy.139
  231.4 0.8 copy.140
  (76 shorter events, 1.7 us)
Async XLA Ops:
  7.2 8.1 %copy-start = (bf16[32,128]{1,0:T(8,128)(2,1)S(1)}, bf16[32,128]{1,0:T(8,128)(2,1)}, u32[]{:S(2)}) copy-start(bf16[32,128]{1,0:T(8,128)(2,1)} %param.8) | copy-start | bytes 24580
  8.8 12.6 %all-to-all-start = ((bf16[4,128,128]{2,0,1:T(4,128)(2,1)}), bf16[4,128,128]{2,0,1:T(4,128)(2,1)S(1)}, u32[]{:S(2)}, u32[]{:S(2)}) async-start(bf16[4,128,128]{2,0,1:T(4,128)(2,1)} %copy.34), calls=%async_computation | async-start | bytes 262144 | tf_op jit(solution)/shard_map/all_to_all | solution.py:44
  31.8 5.5 %collective-permute-start = (bf16[1,128,128]{2,1,0:T(8,128)(2,1)S(1)}, bf16[1,128,128]{2,1,0:T(8,128)(2,1)S(1)}, u32[]{:S(2)}, u32[]{:S(2)}) collective-permute-start(bf16[1,128,128]{2,1,0:T(8,128)(2,1)S(1)} %bitcast.202), channel_id=1, source_target_pairs={{0,4},{4,8},{8,12},{12,16},{16,20},{20,24},{24,28},{28,0},{1,5},{5... | collective-permute-start | bytes 98312 | tf_op jit(solution)/shard_map/ppermute | solution.py:19
  31.9 5.5 %collective-permute-start.1 = (bf16[1,128,128]{2,1,0:T(8,128)(2,1)S(1)}, bf16[1,128,128]{2,1,0:T(8,128)(2,1)S(1)}, u32[]{:S(2)}, u32[]{:S(2)}) collective-permute-start(bf16[1,128,128]{2,1,0:T(8,128)(2,1)S(1)} %bitcast.201), channel_id=1, source_target_pairs={{4,0},{8,4},{12,8},{16,12},{20,16},{24,20},{28,24},{0,28},{5,1},{9... | collective-permute-start | bytes 98312 | tf_op jit(solution)/shard_map/ppermute | solution.py:20
  37.4 6.3 %collective-permute-start.2 = (bf16[6,1,128]{2,1,0:T(2,128)(2,1)S(1)}, bf16[6,1,128]{2,1,0:T(2,128)(2,1)S(1)}, u32[]{:S(2)}, u32[]{:S(2)}) collective-permute-start(bf16[6,1,128]{2,1,0:T(2,128)(2,1)S(1)} %get-tuple-element.41), channel_id=1, source_target_pairs={{0,1},{1,2},{2,3},{3,0},{4,5},{5,6},{6,7},{7,4},{8,9},{9,10},{10,1... | collective-permute-start | bytes 4616 | tf_op jit(solution)/shard_map/ppermute | solution.py:19
  42.9 3.0 %collective-permute-start.3 = (bf16[6,1,128]{2,1,0:T(2,128)(2,1)S(1)}, bf16[6,1,128]{2,1,0:T(2,128)(2,1)S(1)}, u32[]{:S(2)}, u32[]{:S(2)}) collective-permute-start(bf16[6,1,128]{2,1,0:T(2,128)(2,1)S(1)} %get-tuple-element.40), channel_id=1, source_target_pairs={{1,0},{2,1},{3,2},{0,3},{5,4},{6,5},{7,6},{4,7},{9,8},{10,9},{11,1... | collective-permute-start | bytes 4616 | tf_op jit(solution)/shard_map/ppermute | solution.py:20
  46.2 1.0 copy-start.2
  46.2 1.0 copy-start.6
  47.7 6.2 %collective-permute-start.4 = (bf16[2,128,128]{2,1,0:T(8,128)(2,1)S(1)}, bf16[2,128,128]{2,1,0:T(8,128)(2,1)S(1)}, u32[]{:S(2)}, u32[]{:S(2)}) collective-permute-start(bf16[2,128,128]{2,1,0:T(8,128)(2,1)S(1)} %get-tuple-element.46), channel_id=1, source_target_pairs={{0,4},{4,8},{8,12},{12,16},{16,20},{20,24},{24,28},{28,0},{1,5},{5... | collective-permute-start | bytes 196616 | tf_op jit(solution)/shard_map/ppermute | solution.py:19
  47.8 6.1 %collective-permute-start.5 = (bf16[2,128,128]{2,1,0:T(8,128)(2,1)S(1)}, bf16[2,128,128]{2,1,0:T(8,128)(2,1)S(1)}, u32[]{:S(2)}, u32[]{:S(2)}) collective-permute-start(bf16[2,128,128]{2,1,0:T(8,128)(2,1)S(1)} %get-tuple-element.47), channel_id=1, source_target_pairs={{4,0},{8,4},{12,8},{16,12},{20,16},{24,20},{28,24},{0,28},{5,1},{9... | collective-permute-start | bytes 196616 | tf_op jit(solution)/shard_map/ppermute | solution.py:20
  53.9 2.3 collective-permute-start.6
  55.5 3.0 %collective-permute-start.7 = (bf16[8,2,128]{2,1,0:T(2,128)(2,1)S(1)}, bf16[8,2,128]{2,1,0:T(2,128)(2,1)S(1)}, u32[]{:S(2)}, u32[]{:S(2)}) collective-permute-start(bf16[8,2,128]{2,1,0:T(2,128)(2,1)S(1)} %get-tuple-element.26), channel_id=1, source_target_pairs={{1,0},{2,1},{3,2},{0,3},{5,4},{6,5},{7,6},{4,7},{9,8},{10,9},{11,1... | collective-permute-start | bytes 12296 | tf_op jit(solution)/shard_map/ppermute | solution.py:20
  58.6 1.0 copy-start.4
  58.7 1.0 copy-start.7
  58.7 1.0 copy-start.8
  59.1 1.8 copy-start.1
  60.9 5.9 %collective-permute-start.8 = (bf16[2,128,128]{2,1,0:T(8,128)(2,1)S(1)}, bf16[2,128,128]{2,1,0:T(8,128)(2,1)S(1)}, u32[]{:S(2)}, u32[]{:S(2)}) collective-permute-start(bf16[2,128,128]{2,1,0:T(8,128)(2,1)S(1)} %get-tuple-element.44), channel_id=1, source_target_pairs={{0,4},{4,8},{8,12},{12,16},{16,20},{20,24},{24,28},{28,0},{1,5},{5... | collective-permute-start | bytes 196616 | tf_op jit(solution)/shard_map/ppermute | solution.py:19
  61.0 5.9 %collective-permute-start.9 = (bf16[2,128,128]{2,1,0:T(8,128)(2,1)S(1)}, bf16[2,128,128]{2,1,0:T(8,128)(2,1)S(1)}, u32[]{:S(2)}, u32[]{:S(2)}) collective-permute-start(bf16[2,128,128]{2,1,0:T(8,128)(2,1)S(1)} %get-tuple-element.45), channel_id=1, source_target_pairs={{4,0},{8,4},{12,8},{16,12},{20,16},{24,20},{28,24},{0,28},{5,1},{9... | collective-permute-start | bytes 196616 | tf_op jit(solution)/shard_map/ppermute | solution.py:20
  66.9 3.1 %collective-permute-start.10 = (bf16[8,2,128]{2,1,0:T(2,128)(2,1)S(1)}, bf16[8,2,128]{2,1,0:T(2,128)(2,1)S(1)}, u32[]{:S(2)}, u32[]{:S(2)}) collective-permute-start(bf16[8,2,128]{2,1,0:T(2,128)(2,1)S(1)} %get-tuple-element.22), channel_id=1, source_target_pairs={{1,0},{2,1},{3,2},{0,3},{5,4},{6,5},{7,6},{4,7},{9,8},{10,9},{11,1... | collective-permute-start | bytes 12296 | tf_op jit(solution)/shard_map/ppermute | solution.py:20
  66.9 3.0 %collective-permute-start.11 = (bf16[8,2,128]{2,1,0:T(2,128)(2,1)S(1)}, bf16[8,2,128]{2,1,0:T(2,128)(2,1)S(1)}, u32[]{:S(2)}, u32[]{:S(2)}) collective-permute-start(bf16[8,2,128]{2,1,0:T(2,128)(2,1)S(1)} %get-tuple-element.21), channel_id=1, source_target_pairs={{0,1},{1,2},{2,3},{3,0},{4,5},{5,6},{6,7},{7,4},{8,9},{9,10},{10,1... | collective-permute-start | bytes 12296 | tf_op jit(solution)/shard_map/ppermute | solution.py:19
  72.3 6.7 %collective-permute-start.12 = (bf16[1,128,128]{2,1,0:T(8,128)(2,1)}, bf16[1,128,128]{2,1,0:T(8,128)(2,1)S(1)}, u32[]{:S(2)}, u32[]{:S(2)}) collective-permute-start(bf16[1,128,128]{2,1,0:T(8,128)(2,1)} %get-tuple-element.42), channel_id=1, source_target_pairs={{0,4},{4,8},{8,12},{12,16},{16,20},{20,24},{24,28},{28,0},{1,5},{5... | collective-permute-start | bytes 98312 | tf_op jit(solution)/shard_map/ppermute | solution.py:19
  72.3 6.7 %collective-permute-start.13 = (bf16[1,128,128]{2,1,0:T(8,128)(2,1)S(1)}, bf16[1,128,128]{2,1,0:T(8,128)(2,1)S(1)}, u32[]{:S(2)}, u32[]{:S(2)}) collective-permute-start(bf16[1,128,128]{2,1,0:T(8,128)(2,1)S(1)} %get-tuple-element.43), channel_id=1, source_target_pairs={{4,0},{8,4},{12,8},{16,12},{20,16},{24,20},{28,24},{0,28},{5,1},{9... | collective-permute-start | bytes 98312 | tf_op jit(solution)/shard_map/ppermute | solution.py:20
  79.1 3.6 %collective-permute-start.14 = (bf16[6,1,128]{2,1,0:T(2,128)(2,1)S(1)}, bf16[6,1,128]{2,1,0:T(2,128)(2,1)S(1)}, u32[]{:S(2)}, u32[]{:S(2)}) collective-permute-start(bf16[6,1,128]{2,1,0:T(2,128)(2,1)S(1)} %get-tuple-element.37), channel_id=1, source_target_pairs={{1,0},{2,1},{3,2},{0,3},{5,4},{6,5},{7,6},{4,7},{9,8},{10,9},{11,1... | collective-permute-start | bytes 4616 | tf_op jit(solution)/shard_map/ppermute | solution.py:20
  80.6 2.1 collective-permute-start.15
  82.7 1.0 copy-start.5
  84.9 11.4 %all-to-all-start.2 = ((bf16[4,128,128]{2,0,1:T(4,128)(2,1)}), bf16[4,128,128]{2,0,1:T(4,128)(2,1)S(1)}, u32[]{:S(2)}, u32[]{:S(2)}) async-start(bf16[4,128,128]{2,0,1:T(4,128)(2,1)} %copy.46), calls=%async_computation.2 | async-start | bytes 262144 | tf_op jit(solution)/shard_map/all_to_all | solution.py:44
  90.1 139.3 %all-reduce.4.cloned.1.call-start = ((), (), s32[]{:S(2)}) async-start(), calls=%async_computation.3 | async-start | bytes 2359296 | tf_op jit(solution)/shard_map/psum | solution.py:146
  229.4 2.0 copy-start.3
Sparse Core Ops, SparseCore 0:
  97.1 132.2 all-reduce.3
where the time goes:
time: 241 us; the launch traced here: 239 us
  waiting for transfers between devices  114 us (47%)
  blocking collectives  49.2 us (20%)
  starting transfers between devices  40.2 us (17%)
  between operations  14.6 us (6%)
  local copies, waits for them, and re-layouts  11.6 us (5%)
  matrix products  9.08 us (4%)
    psum x1, waiting for transfers between devices, per_device(): lax.psum((second_weight_matrix, bias_two, first_weight_matrix, bias_one,...  91.3 us
    psum x1, blocking collectives, per_device(): lax.psum((second_weight_matrix, bias_two, first_weight_matrix, bias_one,...  40.6 us
    ppermute x8, starting transfers between devices, padded_2(): after = lax.ppermute(leading, axis, down)  18.8 us
    all_to_all x2, starting transfers between devices, to_columns(): return lax.all_to_all(field, 'gx', split_axis=1, concat_axis=0, tiled=True)  11.6 us
    all_to_all x2, waiting for transfers between devices, to_columns(): return lax.all_to_all(field, 'gx', split_axis=1, concat_axis=0, tiled=True)  10.7 us
    ppermute x8, starting transfers between devices, padded_2(): before = lax.ppermute(last, axis, up)  9.79 us
    all_to_all x1, blocking collectives, per_device(): lax.all_to_all(mixed_cols, 'gx', split_axis=0, concat_axis=1, tiled=True)  8.6 us
    unnamed x50, local copies, waits for them, and re-layouts  7.67 us
  transfers between devices with their start and end apart: 19, of which 11 were waited for; matrix products, arithmetic and copies ran while one was open for 3% of the time, Pallas kernels for 0%

commit v1 on v0

v1 whole, which is shorter than its diff:
```python
import functools

import jax
import jax.numpy as jnp
from jax import lax
from jax.experimental import pallas as pl
from jax.experimental.pallas import tpu as pltpu
from jax.sharding import PartitionSpec as P

D1 = 1
D2 = 2
EDGE = 16
BF = jnp.bfloat16
F32 = jnp.float32
MESH = pl.DeviceIdType.MESH


def sigmoid(v):
    return 1.0 / (1.0 + jnp.exp(-v))


def slope_of(v):
    g = sigmoid(v)
    return g * (1.0 + v * (1.0 - g))


def kernel(
    GX, GY, L, WC, C, CH1, CH2,
    lat_in, k_in, w1, b1, w2, b2, cot_in,
    pred, o2, o1, okern, ob1, ob2,
    lat, cot, kd, mix, xf, xs, xh, xg, pre1, hid, wt1, wt2,
    acc1, acc2, hacc1, hacc2, qacc1, qacc2,
    sa1, sa2, ra1, ra2, sb1, sb2, rb1, rb2, sc1, sc2, rc1, rc2, og1, og2,
    ring_s, ring_r, edge_s, edge_r, cot_s, cot_r,
    p1_s, p1_r, p2_s, p2_r, p3_s, p3_r, g3_s, g3_r, g2_s, g2_r, g1_s, g1_r,
):
    NX = L * GX
    W = WC + 2 * EDGE
    GA = GY // 2
    half_n = GX // 2
    gx = lax.axis_index("gx")
    gy = lax.axis_index("gy")
    core = lax.rem(gy, 2)
    ga = gy // 2

    odd = lax.rem(gx, 2)
    pos = (1 - odd) * (gx // 2) + odd * (GX - 1 - gx // 2)

    def at_pos(p):
        p = lax.rem(p + 2 * GX, GX)
        back = (p >= half_n).astype(jnp.int32)
        return (1 - back) * (2 * p) + back * (2 * (GX - 1 - p) + 1)

    right, left = at_pos(pos + 1), at_pos(pos - 1)
    up, down = lax.rem(gx + GX - 1, GX), lax.rem(gx + 1, GX)
    west, east = lax.rem(gy + GY - 1, GY), lax.rem(gy + 1, GY)
    mate = gy + 1 - 2 * core

    barrier = pltpu.get_barrier_semaphore()
    met = 0
    for d in range(1, GX):
        pl.semaphore_signal(barrier, inc=1, device_id=(lax.rem(gx + d, GX), gy), device_id_type=MESH)
        met += 1
    for d in range(1, GY):
        pl.semaphore_signal(barrier, inc=1, device_id=(gx, lax.rem(gy + d, GY)), device_id_type=MESH)
        met += 1
    for vertical in (up, down):
        for side in (west, east):
            pl.semaphore_signal(barrier, inc=1, device_id=(vertical, side), device_id_type=MESH)
            met += 1
    lat[pl.ds(L * gx, L), EDGE : EDGE + WC, :] = lat_in[...]
    pl.semaphore_wait(barrier, met)

    def copy(src, dst, send, recv, target):
        return pltpu.make_async_remote_copy(
            src_ref=src, dst_ref=dst, send_sem=send, recv_sem=recv,
            device_id=target, device_id_type=MESH,
        )

    hl = L // 2

    def ring(way, step, h):
        block = at_pos(pos - (step - 1)) if way == 0 else at_pos(pos + (step - 1))
        piece = lat.at[pl.ds(L * block + h * hl, hl), EDGE : EDGE + WC, :]
        target = (right, gy) if way == 0 else (left, gy)
        where = (way, step - 1, h)
        return copy(piece, piece, ring_s.at[where], ring_r.at[where], target)

    def goes(way, step, h):
        return step < half_n or (step == half_n and h == way)

    def edge(way, block):
        rows = pl.ds(L * block, L)
        if way == 0:
            src, dst, target = lat.at[rows, WC : WC + EDGE, :], lat.at[rows, 0:EDGE, :], (gx, east)
        else:
            src = lat.at[rows, EDGE : 2 * EDGE, :]
            dst, target = lat.at[rows, EDGE + WC : W, :], (gx, west)
        return copy(src, dst, edge_s.at[way, block], edge_r.at[way, block], target)

    for h in range(2):
        for way in range(2):
            ring(way, 1, h).start()
    for way in range(2):
        edge(way, gx).start()

    kd[0:NX, :] = k_in[...].astype(F32)
    kd[NX : 2 * NX, :] = k_in[...].astype(F32)
    cot[3 : 3 + L, EDGE : EDGE + WC, :] = cot_in[...]
    xf[0:8, :] = jnp.zeros((8, C), F32)
    xf[xf.shape[0] - 8 :, :] = jnp.zeros((8, C), F32)
    for p in range(3):
        for q in range(3):
            part = slice(q * C, (q + 1) * C)
            wt1[p, part, :] = w1[p, part, :].astype(F32).T.astype(BF)
            wt2[p, part, :] = w2[p, part, :].astype(F32).T.astype(BF)
    acc1[...] = jnp.zeros(acc1.shape, F32)
    acc2[...] = jnp.zeros(acc2.shape, F32)
    RM = L + 12
    mix[...] = jnp.zeros(mix.shape, F32)
    top = lax.rem(L * gx - 6 + 2 * NX, NX)

    def correlate(rows_at, count, tiles):
        base = lax.rem(rows_at - top + 2 * NX, NX)

        def tile(t, carry):
            col = pl.multiple_of(tiles[0] + t * tiles[1], 16)
            parts = [mix[m, pl.ds(col, 16), :] for m in range(RM)]
            for r in range(count):
                row = lax.rem(base + r, NX)
                value = lat[rows_at + r, pl.ds(col, 16), :].astype(F32)
                for m in range(RM):
                    factor = kd[pl.ds(lax.rem(row + (2 * NX - m), NX), 1), :]
                    parts[m] = parts[m] + value * factor
            for m in range(RM):
                mix[m, pl.ds(col, 16), :] = parts[m]
            return carry

        lax.fori_loop(0, tiles[2], tile, 0)

    center = (EDGE, 16, WC // 16)
    sides = (0, EDGE + WC, 2)
    correlate(L * gx, L, center)

    def cot_copy(i):
        rows_src = (slice(L - 3, L), slice(0, L), slice(0, 3))
        rows_dst = (slice(0, 3), slice(3, 3 + L), slice(3 + L, 6 + L))
        cols_src = (slice(WC - EDGE, WC), slice(0, WC), slice(0, EDGE))
        cols_dst = (slice(0, EDGE), slice(EDGE, EDGE + WC), slice(EDGE + WC, W))
        a, b = i // 3, i % 3
        target = ((down, gx, up)[a], (east, gy, west)[b])
        return copy(
            cot_in.at[rows_src[a], cols_src[b], :], cot.at[rows_dst[a], cols_dst[b], :],
            cot_s.at[i], cot_r.at[i], target,
        )

    cots = [i for i in range(9) if i != 4]
    for step in range(1, half_n + 1):
        for h in range(2):
            for way in range(2):
                if goes(way, step, h):
                    ring(way, step, h).wait_recv()
                    if goes(way, step + 1, h):
                        ring(way, step + 1, h).start()
        if step < half_n:
            blocks = [at_pos(pos - step), at_pos(pos + step)]
        else:
            blocks = [at_pos(pos + step)]
        for block in blocks:
            for way in range(2):
                edge(way, block).start()
        if step == half_n:
            for i in cots:
                cot_copy(i).start()
        for block in blocks:
            correlate(L * block, L, center)

    def late(block, carry):
        for way in range(2):
            edge(way, block).wait_recv()
        return carry

    lax.fori_loop(0, GX, late, 0)

    def late_rows(block, carry):
        correlate(L * block, L, sides)
        return carry

    lax.fori_loop(0, GX, late_rows, 0)

    def flat(ref):
        return ref[...].reshape(-1, C)

    def widen(target, value, rows, dil):
        m = rows * W
        xf[8 : 8 + m, :] = value
        for q in range(3):
            at = 8 + (q - 1) * dil
            target[0:m, q * C : (q + 1) * C] = xf[at : at + m, :].astype(BF)

    def rows_dot(source, starts, weight, rows):
        total = None
        for p in range(3):
            at = starts[p] * W
            term = jnp.dot(source[at : at + rows * W, :], weight[p], preferred_element_type=F32)
            total = term if total is None else total + term
        return total

    def weight_grad(source, starts, slope_own, p):
        at = starts[p]
        taps = jnp.concatenate(
            [source[(at + i) * W + EDGE : (at + i) * W + EDGE + WC, :] for i in range(L)], axis=0
        )
        return lax.dot_general(taps, slope_own, (((0,), (0,)), ((), ())), preferred_element_type=F32)

    def own(value, start):
        return jnp.concatenate(
            [value[(start + i) * W + EDGE : (start + i) * W + EDGE + WC, :] for i in range(L)], axis=0
        )

    for m in range(RM):
        row = lat[lax.rem(top + m, NX), :, :].astype(F32)
        mix[m] = (row + mix[m]).astype(BF).astype(F32)

    R1 = L + 10
    widen(xs, flat(mix), RM, D1)
    pre1[...] = rows_dot(xs, (0, 1, 2), w1, R1) + b1[...]
    v = pre1[...]
    mixed_in = mix[1 : 1 + R1].reshape(-1, C)
    hid[...] = (mixed_in + v * sigmoid(v)).astype(BF).astype(F32)
    R2 = L + 6
    widen(xh, hid[...], R1, D2)
    pre2 = rows_dot(xh, (0, 2, 4), w2, R2) + b2[...]
    own2 = own(pre2, 3)
    own_hid = own(hid, 5)
    pred[...] = (own_hid + own2 * sigmoid(own2)).astype(BF).reshape(L, WC, C)
    for i in cots:
        cot_copy(i).wait_recv()
    slope2 = (flat(cot).astype(F32) * slope_of(pre2)).astype(BF).astype(F32)
    own_slope2 = own(slope2, 3)
    grad2 = [weight_grad(xh, (3, 5, 7), own_slope2.astype(BF), p) for p in range(3)]
    SIZE = 9 * C
    first = min(acc1.shape[0], SIZE)

    def put_second(p):
        lo, hi = p * 3 * C, (p + 1) * 3 * C
        cut = min(max(first, lo), hi)
        if cut > lo:
            acc1[lo:cut, :] = grad2[p][: cut - lo]
        if cut < hi:
            acc2[cut - first : hi - first, :] = grad2[p][cut - lo :]

    for p in range(3):
        put_second(p)

    class Stream:
        pass

    streams = []
    for k in range(2):
        s = Stream()
        s.k = k
        s.ch = (CH1, CH2)[k]
        s.acc, s.hacc, s.qacc = (acc1, acc2)[k], (hacc1, hacc2)[k], (qacc1, qacc2)[k]
        s.sa, s.ra = (sa1, sa2)[k], (ra1, ra2)[k]
        s.sb, s.rb = (sb1, sb2)[k], (rb1, rb2)[k]
        s.sc, s.rc, s.og = (sc1, sc2)[k], (rc1, rc2)[k], (og1, og2)[k]
        s.quarter = GX * s.ch
        s.half = GA * s.quarter
        streams.append(s)

    def ds(at, size):
        return pl.ds(pl.multiple_of(at, 16), size)

    def p1(s):
        return copy(s.sa, s.ra, p1_s.at[s.k], p1_r.at[s.k], (gx, mate))

    def p2(s, d):
        other = lax.rem(ga + d, GA)
        return copy(s.sb.at[ds(other * s.quarter, s.quarter), :], s.rb.at[d],
                    p2_s.at[s.k, d], p2_r.at[s.k, d], (gx, 2 * other + core))

    def p3(s, d):
        other = lax.rem(gx + d, GX)
        return copy(s.sc.at[ds(other * s.ch, s.ch), :], s.rc.at[d],
                    p3_s.at[s.k, d], p3_r.at[s.k, d], (other, gy))

    def g3(s, d, send):
        owner = gx if send else lax.rem(gx + GX - d, GX)
        piece = s.og.at[ds(core * s.half + ga * s.quarter + owner * s.ch, s.ch), :]
        return copy(piece, piece, g3_s.at[s.k, d], g3_r.at[s.k, d], (lax.rem(gx + d, GX), gy))

    def g2(s, d, send):
        owner = ga if send else lax.rem(ga + GA - d, GA)
        piece = s.og.at[ds(core * s.half + owner * s.quarter, s.quarter), :]
        return copy(piece, piece, g2_s.at[s.k, d], g2_r.at[s.k, d],
                    (gx, 2 * lax.rem(ga + d, GA) + core))

    def g1(s, send):
        owner = core if send else 1 - core
        piece = s.og.at[ds(owner * s.half, s.half), :]
        return copy(piece, piece, g1_s.at[s.k], g1_r.at[s.k], (gx, mate))

    def begin(s):
        s.sa[...] = s.acc[ds((1 - core) * s.half, s.half), :].astype(BF)
        p1(s).start()

    def after_one(s):
        p1(s).wait_recv()
        total = s.acc[ds(core * s.half, s.half), :] + s.ra[...].astype(F32)
        s.hacc[...] = total
        s.sb[...] = total.astype(BF)
        for d in range(1, GA):
            p2(s, d).start()

    def after_two(s):
        total = s.hacc[ds(ga * s.quarter, s.quarter), :]
        for d in range(1, GA):
            p2(s, d).wait_recv()
            total = total + s.rb[d].astype(F32)
        s.qacc[...] = total
        s.sc[...] = total.astype(BF)
        for d in range(1, GX):
            p3(s, d).start()

    def after_three(s):
        total = s.qacc[ds(gx * s.ch, s.ch), :]
        for d in range(1, GX):
            p3(s, d).wait_recv()
            total = total + s.rc[d].astype(F32)
        s.og[ds(core * s.half + ga * s.quarter + gx * s.ch, s.ch), :] = total.astype(BF)
        for d in range(1, GX):
            g3(s, d, True).start()

    def gather_two(s):
        for d in range(1, GX):
            g3(s, d, False).wait_recv()
        for d in range(1, GA):
            g2(s, d, True).start()

    def gather_one(s):
        for d in range(1, GA):
            g2(s, d, False).wait_recv()
        g1(s, True).start()

    one, two = streams
    begin(one)

    R3 = L + 2
    widen(xg, slope2, R2, -D2)
    back2 = rows_dot(xg, (4, 2, 0), wt2, R3)
    grad_hid = flat(cot)[2 * W : (2 + R3) * W].astype(F32) + back2
    slope1 = (grad_hid * slope_of(pre1[4 * W : (4 + R3) * W, :])).astype(BF).astype(F32)
    after_one(one)
    own_slope1 = own(slope1, 1)
    shift = SIZE - first
    for p in range(3):
        lo = shift + p * 3 * C
        acc2[lo : lo + 3 * C, :] = weight_grad(xs, (5, 6, 7), own_slope1.astype(BF), p)
    widen(xg, slope1, R3, -D1)
    grad_mixed = grad_hid[W : (1 + L) * W] + rows_dot(xg, (2, 1, 0), wt1, L)
    mix[0:L, EDGE : EDGE + WC, :] = own(grad_mixed, 0).astype(BF).astype(F32).reshape(L, WC, C)
    misc = shift + SIZE

    def kernel_row(o, carry):
        total = jnp.zeros((16, C), F32)
        for i in range(L):
            row = lax.rem(L * gx + i + o, NX)
            for t in range(WC // 16):
                cols = slice(EDGE + t * 16, EDGE + (t + 1) * 16)
                total = total + mix[i, cols, :] * lat[row, cols, :].astype(F32)
        acc2[pl.ds(misc + o, 1), :] = jnp.sum(total, axis=0, keepdims=True)
        return carry

    lax.fori_loop(0, NX, kernel_row, 0)
    acc2[misc + NX : misc + NX + 1, :] = jnp.sum(own_slope1, axis=0, keepdims=True)
    acc2[misc + NX + 8 : misc + NX + 9, :] = jnp.sum(own_slope2, axis=0, keepdims=True)

    begin(two)
    after_two(one)
    after_one(two)
    after_three(one)
    after_two(two)
    gather_two(one)
    after_three(two)
    gather_one(one)
    gather_two(two)
    gather_one(two)
    g1(one, False).wait_recv()
    o2[0:first, :] = og1[0:first, :]
    g1(two, False).wait_recv()
    if first < SIZE:
        o2[first:SIZE, :] = og2[0:shift, :]
    o1[...] = og2[shift : shift + SIZE, :]
    okern[...] = og2[misc : misc + NX, :].astype(F32)
    tail = og2[misc + NX : misc + NX + 16, :].astype(F32)
    ob1[...] = tail[0:1]
    ob2[...] = tail[8:9]

    for step in range(1, half_n + 1):
        for h in range(2):
            for way in range(2):
                if goes(way, step, h):
                    ring(way, step, h).wait_send()

    def sent(block, carry):
        for way in range(2):
            edge(way, block).wait_send()
        return carry

    lax.fori_loop(0, GX, sent, 0)
    for i in cots:
        cot_copy(i).wait_send()
    for s in streams:
        p1(s).wait_send()
        for d in range(1, GA):
            p2(s, d).wait_send()
            g2(s, d, True).wait_send()
        for d in range(1, GX):
            p3(s, d).wait_send()
            g3(s, d, True).wait_send()
        g1(s, True).wait_send()


def per_device(latent, corr_kernel, w1, b1, w2, b2, cotangent):
    GX, GY = lax.axis_size("gx"), lax.axis_size("gy")
    L, WC, C = latent.shape
    NX = L * GX
    W = WC + 2 * EDGE
    N = GX * GY
    GA = GY // 2
    SIZE = 9 * C
    CH1 = max(16, SIZE // (16 * N) * 16)
    rest = SIZE - min(SIZE, CH1 * N) + SIZE + NX + 16
    CH2 = -(-rest // (16 * N)) * 16
    dma = pltpu.SemaphoreType.DMA

    def pair(shape_of, kind):
        return [pltpu.VMEM(shape_of(ch), kind) for ch in (CH1, CH2)]

    scratch = [
        pltpu.VMEM((NX, W, C), BF),
        pltpu.VMEM((L + 6, W, C), BF),
        pltpu.VMEM((2 * NX, C), F32),
        pltpu.VMEM((L + 12, W, C), F32),
        pltpu.VMEM(((L + 12) * W + 16, C), F32),
        pltpu.VMEM(((L + 12) * W, 3 * C), BF),
        pltpu.VMEM(((L + 10) * W, 3 * C), BF),
        pltpu.VMEM(((L + 6) * W, 3 * C), BF),
        pltpu.VMEM(((L + 10) * W, C), F32),
        pltpu.VMEM(((L + 10) * W, C), F32),
        pltpu.VMEM((3, 3 * C, C), BF),
        pltpu.VMEM((3, 3 * C, C), BF),
        *pair(lambda ch: (N * ch, C), F32),
        *pair(lambda ch: (GA * GX * ch, C), F32),
        *pair(lambda ch: (GX * ch, C), F32),
        *pair(lambda ch: (GA * GX * ch, C), BF),
        *pair(lambda ch: (GA * GX * ch, C), BF),
        *pair(lambda ch: (GA * GX * ch, C), BF),
        *pair(lambda ch: (GA, GX * ch, C), BF),
        *pair(lambda ch: (GX * ch, C), BF),
        *pair(lambda ch: (GX, ch, C), BF),
        *pair(lambda ch: (N * ch, C), BF),
        dma((2, GX // 2, 2)), dma((2, GX // 2, 2)),
        dma((2, GX)), dma((2, GX)),
        dma((9,)), dma((9,)),
        dma((2,)), dma((2,)),
        dma((2, GA)), dma((2, GA)),
        dma((2, GX)), dma((2, GX)),
        dma((2, GX)), dma((2, GX)),
        dma((2, GA)), dma((2, GA)),
        dma((2,)), dma((2,)),
    ]
    vmem = pl.BlockSpec(memory_space=pltpu.VMEM)
    pred, g2, g1, gk, gb1, gb2 = pl.pallas_call(
        functools.partial(kernel, GX, GY, L, WC, C, CH1, CH2),
        out_shape=(
            jax.ShapeDtypeStruct((L, WC, C), BF),
            jax.ShapeDtypeStruct((SIZE, C), BF),
            jax.ShapeDtypeStruct((SIZE, C), BF),
            jax.ShapeDtypeStruct((NX, C), F32),
            jax.ShapeDtypeStruct((1, C), F32),
            jax.ShapeDtypeStruct((1, C), F32),
        ),
        in_specs=[vmem] * 7,
        out_specs=[vmem] * 6,
        scratch_shapes=scratch,
        compiler_params=pltpu.CompilerParams(
            collective_id=0, has_side_effects=True, vmem_limit_bytes=56 * 1024 * 1024
        ),
        cost_estimate=pl.CostEstimate(
            flops=2 * 6 * 10 * W * SIZE * C, bytes_accessed=4 * SIZE * C * 2, transcendentals=24 * W * C
        ),
    )(
        latent, corr_kernel, w1.reshape(3, 3 * C, C), b1.reshape(1, C),
        w2.reshape(3, 3 * C, C), b2.reshape(1, C), cotangent,
    )
    shape = (3, 3, C, C)
    return (
        pred,
        g1.astype(F32).reshape(shape), gb1.reshape(C),
        g2.astype(F32).reshape(shape), gb2.reshape(C),
        gk,
    )


def solution(mesh):
    in_specs = (P("gx", "gy", None), P(), P(), P(), P(), P(), P("gx", "gy", None))
    out_specs = (P("gx", "gy", None), P(), P(), P(), P(), P())
    return jax.shard_map(
        per_device, mesh=mesh, in_specs=in_specs, out_specs=out_specs, check_vma=False
    )
```

time: 241 us -> 63.8 us (0.26)
  waiting for transfers between devices: 114 us -> 0 us
  Pallas kernels: 0 us -> 57.8 us
  blocking collectives: 49.2 us -> 0 us
  starting transfers between devices: 40.2 us -> 0 us
  between operations: 14.6 us -> 0.66 us
  local copies, waits for them, and re-layouts: 11.6 us -> 2.45 us
  matrix products: 9.08 us -> 0 us
    psum x1 -> x0, waiting for transfers between devices: 91.3 us -> none  [per_device(): lax.psum((second_weight_matrix, bias_two, first_weight_matrix, bias_one,...]
    pallas_call x0 -> x1, Pallas kernels: none -> 57.8 us  [per_device(): pl.pallas_call(functools.partial(kernel, GX, GY, L, WC, C, CH1, CH2), out...]
    psum x1 -> x0, blocking collectives: 40.6 us -> none  [per_device(): lax.psum((second_weight_matrix, bias_two, first_weight_matrix, bias_one,...]
    ppermute x16 -> x0, starting transfers between devices: 28.6 us -> none  [the longest x8 18.8 us: padded_2(): after = lax.ppermute(leading, axis, down)]
    ppermute x16 -> x0, waiting for transfers between devices: 11.6 us -> none  [the longest x8 5.95 us: padded_2(): before = lax.ppermute(last, axis, up)]
    all_to_all x2 -> x0, starting transfers between devices: 11.6 us -> none  [to_columns(): return lax.all_to_all(field, 'gx', split_axis=1, concat_axis=0, tiled=True)]
    all_to_all x2 -> x0, waiting for transfers between devices: 10.7 us -> none  [to_columns(): return lax.all_to_all(field, 'gx', split_axis=1, concat_axis=0, tiled=True)]
    dot_general x16 -> x0, matrix products: 9.08 us -> none  [the longest x10 3.08 us: transform(): jnp.dot(table_mat, operand, precision=lax.Precision.HIGHEST, preferred_el...]
  transfers between devices with their start and end apart: 19 -> 0, of which waited for: 11 -> 0; matrix products, arithmetic and copies ran while one was open for 3% -> 0% of each run, Pallas kernels for 0% -> 0%
where the time goes in v1:
time: 63.8 us; the launch traced here: 63.6 us
  Pallas kernels  57.8 us (91%)
  other arithmetic  2.73 us (4%)
  local copies, waits for them, and re-layouts  2.45 us (4%)
  between operations  0.66 us (1%)
    pallas_call x1, Pallas kernels, per_device(): pl.pallas_call(functools.partial(kernel, GX, GY, L, WC, C, CH1, CH2), out...  57.8 us
    unnamed x14, local copies, waits for them, and re-layouts  2.45 us
    reshape x1, other arithmetic, per_device(): g1.astype(F32).reshape(shape)  1.87 us

profile of v1, /device:TPU:1, one launch (start us, length us, event | category | flops | bytes accessed | tf_op | source)
XLA Modules:
  0.0 63.6 jit_solution(275446944124098050)
XLA Ops:
  0.6 57.8 %shard_map.118 = (bf16[4,128,128]{2,1,0:T(8,128)(2,1)}, bf16[1152,128]{1,0:T(8,128)(2,1)}, bf16[1152,128]{1,0:T(8,128)(2,1)}, f32[32,128]{1,0:T(8,128)}, f32[1,128]{1,0:T(1,128)}, /*index=5*/f32[1,128]{1,0:T(1,128)}) custom-call(bf16[4,128,128]{2,1,0:T(8,128)(2,1)} %lat_in.1, bf16[32,128]{1,0:T(8,128)(2,1)} %k_in.1, bf16[3,384,128]{2,1,0:T(8,128)(2,1)} %bitcast.12, ...), custom_call_target="tpu_custom_call" | custom-call | flops 2831155200 | bytes 1179648 | tf_op jit(solution)/shard_map/pallas_call | solution.py:475
  58.4 0.0 copy-start
  58.4 1.9 %convert.2 = f32[3,3,128,128]{3,2,1,0:T(8,128)} convert(bf16[3,3,128,128]{3,2,1,0:T(8,128)(2,1)} %bitcast.11) | non-fusion elementwise | flops 147456 | bytes 884736 | tf_op jit(solution)/shard_map/reshape | solution.py:501
  60.3 0.0 copy-done
  60.3 0.0 copy-start.1
  60.3 0.9 %convert.3 = f32[3,3,128,128]{3,2,1,0:T(8,128)} convert(bf16[3,3,128,128]{3,2,1,0:T(8,128)(2,1)S(1)} %bitcast.10) | non-fusion elementwise | flops 147456 | bytes 884736 | tf_op jit(solution)/shard_map/reshape | solution.py:502
  61.1 0.0 copy-done.1
  61.2 0.0 copy-start.4
  61.2 0.0 copy-start.2
  61.2 0.7 %copy.17 = bf16[4,128,128]{2,1,0:T(8,128)(2,1)} copy(bf16[4,128,128]{2,1,0:T(8,128)(2,1)S(1)} %copy-done.1) | data formatting | bytes 262144
  61.8 0.0 copy-done.4
  61.9 0.0 copy-start.3
  61.9 0.5 copy.18
  62.4 0.1 copy-done.3
  62.5 0.5 copy.19
  63.0 0.0 copy-done.2
  63.0 0.6 copy.20
Async XLA Ops:
  58.4 1.9 %copy-start = (bf16[1152,128]{1,0:T(8,128)(2,1)S(1)}, bf16[1152,128]{1,0:T(8,128)(2,1)}, u32[]{:S(2)}) copy-start(bf16[1152,128]{1,0:T(8,128)(2,1)} %get-tuple-element.15) | copy-start | bytes 884740
  60.3 0.9 %copy-start.1 = (bf16[4,128,128]{2,1,0:T(8,128)(2,1)S(1)}, bf16[4,128,128]{2,1,0:T(8,128)(2,1)}, u32[]{:S(2)}) copy-start(bf16[4,128,128]{2,1,0:T(8,128)(2,1)} %get-tuple-element.24) | copy-start | bytes 393220
  61.2 0.7 %copy-start.4 = (f32[1,128]{1,0:T(1,128)S(1)}, f32[1,128]{1,0:T(1,128)}, u32[]{:S(2)}) copy-start(f32[1,128]{1,0:T(1,128)} %get-tuple-element.14) | copy-start | bytes 1540
  61.2 1.8 %copy-start.2 = (f32[32,128]{1,0:T(8,128)S(1)}, f32[32,128]{1,0:T(8,128)}, u32[]{:S(2)}) copy-start(f32[32,128]{1,0:T(8,128)} %get-tuple-element.29) | copy-start | bytes 49156
  61.9 0.6 copy-start.3

commit v2 on v1

--- a/solution.py
+++ b/solution.py
@@ -27,7 +27,7 @@
 def kernel(
     GX, GY, L, WC, C, CH1, CH2,
     lat_in, k_in, w1, b1, w2, b2, cot_in,
-    pred, o2, o1, okern, ob1, ob2,
+    pred, o2, o1, orest,
     lat, cot, kd, mix, xf, xs, xh, xg, pre1, hid, wt1, wt2,
     acc1, acc2, hacc1, hacc2, qacc1, qacc2,
     sa1, sa2, ra1, ra2, sb1, sb2, rb1, rb2, sc1, sc2, rc1, rc2, og1, og2,
@@ -104,18 +104,28 @@
     for way in range(2):
         edge(way, gx).start()
 
-    kd[0:NX, :] = k_in[...].astype(F32)
-    kd[NX : 2 * NX, :] = k_in[...].astype(F32)
+    spread = jnp.broadcast_to(k_in[...].astype(F32)[:, None, :], (NX, 8, C))
+    for i in range(3):
+        kd[i * NX : (i + 1) * NX, :, :] = spread
     cot[3 : 3 + L, EDGE : EDGE + WC, :] = cot_in[...]
     xf[0:8, :] = jnp.zeros((8, C), F32)
     xf[xf.shape[0] - 8 :, :] = jnp.zeros((8, C), F32)
-    for p in range(3):
-        for q in range(3):
-            part = slice(q * C, (q + 1) * C)
-            wt1[p, part, :] = w1[p, part, :].astype(F32).T.astype(BF)
-            wt2[p, part, :] = w2[p, part, :].astype(F32).T.astype(BF)
-    acc1[...] = jnp.zeros(acc1.shape, F32)
-    acc2[...] = jnp.zeros(acc2.shape, F32)
+
+    def turn(target, weight):
+        for p in range(3):
+            for q in range(3):
+                from_at, to_at = (3 * p + q) * C, (3 * (2 - p) + q) * C
+                target[to_at : to_at + C, :] = weight[from_at : from_at + C, :].astype(F32).T.astype(BF)
+
+    def prepare(step):
+        if step == 1:
+            turn(wt2, w2)
+        if step == min(2, half_n):
+            turn(wt1, w1)
+        if step == min(3, half_n):
+            acc1[...] = jnp.zeros(acc1.shape, F32)
+            acc2[...] = jnp.zeros(acc2.shape, F32)
+
     RM = L + 12
     mix[...] = jnp.zeros(mix.shape, F32)
     top = lax.rem(L * gx - 6 + 2 * NX, NX)
@@ -125,15 +135,18 @@
 
         def tile(t, carry):
             col = pl.multiple_of(tiles[0] + t * tiles[1], 16)
-            parts = [mix[m, pl.ds(col, 16), :] for m in range(RM)]
+            parts = [
+                [mix[m, pl.ds(pl.multiple_of(col + 8 * e, 8), 8), :] for e in range(2)] for m in range(RM)
+            ]
+            factors = {d: kd[base + (NX + d)] for d in range(1 - RM, count)}
             for r in range(count):
-                row = lax.rem(base + r, NX)
                 value = lat[rows_at + r, pl.ds(col, 16), :].astype(F32)
                 for m in range(RM):
-                    factor = kd[pl.ds(lax.rem(row + (2 * NX - m), NX), 1), :]
-                    parts[m] = parts[m] + value * factor
+                    for e in range(2):
+                        parts[m][e] = parts[m][e] + value[8 * e : 8 * e + 8] * factors[r - m]
             for m in range(RM):
-                mix[m, pl.ds(col, 16), :] = parts[m]
+                for e in range(2):
+                    mix[m, pl.ds(pl.multiple_of(col + 8 * e, 8), 8), :] = parts[m][e]
             return carry
 
         lax.fori_loop(0, tiles[2], tile, 0)
@@ -154,6 +167,12 @@
             cot_s.at[i], cot_r.at[i], target,
         )
 
+    def add_edges(block):
+        for way in range(2):
+            edge(way, block).wait_recv()
+        correlate(L * block, L, sides)
+
+    waiting = [gx]
     cots = [i for i in range(9) if i != 4]
     for step in range(1, half_n + 1):
         for h in range(2):
@@ -174,19 +193,12 @@
                 cot_copy(i).start()
         for block in blocks:
             correlate(L * block, L, center)
-
-    def late(block, carry):
-        for way in range(2):
-            edge(way, block).wait_recv()
-        return carry
-
-    lax.fori_loop(0, GX, late, 0)
-
-    def late_rows(block, carry):
-        correlate(L * block, L, sides)
-        return carry
-
-    lax.fori_loop(0, GX, late_rows, 0)
+        for block in waiting:
+            add_edges(block)
+        waiting = blocks
+        prepare(step)
+    for block in waiting:
+        add_edges(block)
 
     def flat(ref):
         return ref[...].reshape(-1, C)
@@ -199,12 +211,8 @@
             target[0:m, q * C : (q + 1) * C] = xf[at : at + m, :].astype(BF)
 
     def rows_dot(source, starts, weight, rows):
-        total = None
-        for p in range(3):
-            at = starts[p] * W
-            term = jnp.dot(source[at : at + rows * W, :], weight[p], preferred_element_type=F32)
-            total = term if total is None else total + term
-        return total
+        taps = jnp.concatenate([source[at * W : (at + rows) * W, :] for at in starts], axis=1)
+        return jnp.dot(taps, weight[...], preferred_element_type=F32)
 
     def weight_grad(source, starts, slope_own, p):
         at = starts[p]
@@ -348,7 +356,7 @@
 
     R3 = L + 2
     widen(xg, slope2, R2, -D2)
-    back2 = rows_dot(xg, (4, 2, 0), wt2, R3)
+    back2 = rows_dot(xg, (0, 2, 4), wt2, R3)
     grad_hid = flat(cot)[2 * W : (2 + R3) * W].astype(F32) + back2
     slope1 = (grad_hid * slope_of(pre1[4 * W : (4 + R3) * W, :])).astype(BF).astype(F32)
     after_one(one)
@@ -358,21 +366,28 @@
         lo = shift + p * 3 * C
         acc2[lo : lo + 3 * C, :] = weight_grad(xs, (5, 6, 7), own_slope1.astype(BF), p)
     widen(xg, slope1, R3, -D1)
-    grad_mixed = grad_hid[W : (1 + L) * W] + rows_dot(xg, (2, 1, 0), wt1, L)
+    grad_mixed = grad_hid[W : (1 + L) * W] + rows_dot(xg, (0, 1, 2), wt1, L)
     mix[0:L, EDGE : EDGE + WC, :] = own(grad_mixed, 0).astype(BF).astype(F32).reshape(L, WC, C)
     misc = shift + SIZE
 
-    def kernel_row(o, carry):
-        total = jnp.zeros((16, C), F32)
-        for i in range(L):
-            row = lax.rem(L * gx + i + o, NX)
-            for t in range(WC // 16):
-                cols = slice(EDGE + t * 16, EDGE + (t + 1) * 16)
-                total = total + mix[i, cols, :] * lat[row, cols, :].astype(F32)
-        acc2[pl.ds(misc + o, 1), :] = jnp.sum(total, axis=0, keepdims=True)
+    def kernel_rows(part, carry):
+        base = L * gx + 4 * part
+        totals = [jnp.zeros((8, C), F32) for _ in range(4)]
+        rows = [lax.rem(base + i, NX) for i in range(L + 3)]
+        for t in range(WC // 16):
+            cols = slice(EDGE + t * 16, EDGE + (t + 1) * 16)
+            fields = [lat[row, cols, :].astype(F32) for row in rows]
+            for i in range(L):
+                for e in range(2):
+                    at = EDGE + t * 16 + 8 * e
+                    grad = mix[i, at : at + 8, :]
+                    for o in range(4):
+                        totals[o] = totals[o] + grad * fields[i + o][8 * e : 8 * e + 8]
+        for o in range(4):
+            acc2[pl.ds(misc + 4 * part + o, 1), :] = jnp.sum(totals[o], axis=0, keepdims=True)
         return carry
 
-    lax.fori_loop(0, NX, kernel_row, 0)
+    lax.fori_loop(0, NX // 4, kernel_rows, 0)
     acc2[misc + NX : misc + NX + 1, :] = jnp.sum(own_slope1, axis=0, keepdims=True)
     acc2[misc + NX + 8 : misc + NX + 9, :] = jnp.sum(own_slope2, axis=0, keepdims=True)
 
@@ -392,10 +407,7 @@
     if first < SIZE:
         o2[first:SIZE, :] = og2[0:shift, :]
     o1[...] = og2[shift : shift + SIZE, :]
-    okern[...] = og2[misc : misc + NX, :].astype(F32)
-    tail = og2[misc + NX : misc + NX + 16, :].astype(F32)
-    ob1[...] = tail[0:1]
-    ob2[...] = tail[8:9]
+    orest[...] = og2[misc : misc + NX + 16, :]
 
     for step in range(1, half_n + 1):
         for h in range(2):
@@ -422,6 +434,16 @@
         g1(s, True).wait_send()
 
 
+def closing(NX, pred, o2, o1, rest, pred_out, g1, gb1, g2, gb2, gk):
+    pred_out[...] = pred[...]
+    g1[...] = o1[...].astype(F32)
+    g2[...] = o2[...].astype(F32)
+    gk[...] = rest[0:NX, :].astype(F32)
+    tail = rest[NX : NX + 16, :].astype(F32)
+    gb1[...] = tail[0:1]
+    gb2[...] = tail[8:9]
+
+
 def per_device(latent, corr_kernel, w1, b1, w2, b2, cotangent):
     GX, GY = lax.axis_size("gx"), lax.axis_size("gy")
     L, WC, C = latent.shape
@@ -441,7 +463,7 @@
     scratch = [
         pltpu.VMEM((NX, W, C), BF),
         pltpu.VMEM((L + 6, W, C), BF),
-        pltpu.VMEM((2 * NX, C), F32),
+        pltpu.VMEM((3 * NX, 8, C), F32),
         pltpu.VMEM((L + 12, W, C), F32),
         pltpu.VMEM(((L + 12) * W + 16, C), F32),
         pltpu.VMEM(((L + 12) * W, 3 * C), BF),
@@ -449,8 +471,8 @@
         pltpu.VMEM(((L + 6) * W, 3 * C), BF),
         pltpu.VMEM(((L + 10) * W, C), F32),
         pltpu.VMEM(((L + 10) * W, C), F32),
-        pltpu.VMEM((3, 3 * C, C), BF),
-        pltpu.VMEM((3, 3 * C, C), BF),
+        pltpu.VMEM((9 * C, C), BF),
+        pltpu.VMEM((9 * C, C), BF),
         *pair(lambda ch: (N * ch, C), F32),
         *pair(lambda ch: (GA * GX * ch, C), F32),
         *pair(lambda ch: (GX * ch, C), F32),
@@ -472,18 +494,16 @@
         dma((2,)), dma((2,)),
     ]
     vmem = pl.BlockSpec(memory_space=pltpu.VMEM)
-    pred, g2, g1, gk, gb1, gb2 = pl.pallas_call(
+    held = pl.pallas_call(
         functools.partial(kernel, GX, GY, L, WC, C, CH1, CH2),
         out_shape=(
             jax.ShapeDtypeStruct((L, WC, C), BF),
             jax.ShapeDtypeStruct((SIZE, C), BF),
             jax.ShapeDtypeStruct((SIZE, C), BF),
-            jax.ShapeDtypeStruct((NX, C), F32),
-            jax.ShapeDtypeStruct((1, C), F32),
-            jax.ShapeDtypeStruct((1, C), F32),
+            jax.ShapeDtypeStruct((NX + 16, C), BF),
         ),
         in_specs=[vmem] * 7,
-        out_specs=[vmem] * 6,
+        out_specs=[vmem] * 4,
         scratch_shapes=scratch,
         compiler_params=pltpu.CompilerParams(
             collective_id=0, has_side_effects=True, vmem_limit_bytes=56 * 1024 * 1024
@@ -492,16 +512,25 @@
             flops=2 * 6 * 10 * W * SIZE * C, bytes_accessed=4 * SIZE * C * 2, transcendentals=24 * W * C
         ),
     )(
-        latent, corr_kernel, w1.reshape(3, 3 * C, C), b1.reshape(1, C),
-        w2.reshape(3, 3 * C, C), b2.reshape(1, C), cotangent,
+        latent, corr_kernel, w1.reshape(9 * C, C), b1.reshape(1, C),
+        w2.reshape(9 * C, C), b2.reshape(1, C), cotangent,
     )
+    pred, g1, gb1, g2, gb2, gk = pl.pallas_call(
+        functools.partial(closing, NX),
+        out_shape=(
+            jax.ShapeDtypeStruct((L, WC, C), BF),
+            jax.ShapeDtypeStruct((SIZE, C), F32),
+            jax.ShapeDtypeStruct((1, C), F32),
+            jax.ShapeDtypeStruct((SIZE, C), F32),
+            jax.ShapeDtypeStruct((1, C), F32),
+            jax.ShapeDtypeStruct((NX, C), F32),
+        ),
+        in_specs=[vmem] * 4,
+        out_specs=[vmem] * 6,
+        compiler_params=pltpu.CompilerParams(vmem_limit_bytes=16 * 1024 * 1024),
+    )(*held)
     shape = (3, 3, C, C)
-    return (
-        pred,
-        g1.astype(F32).reshape(shape), gb1.reshape(C),
-        g2.astype(F32).reshape(shape), gb2.reshape(C),
-        gk,
-    )
+    return (pred, g1.reshape(shape), gb1.reshape(C), g2.reshape(shape), gb2.reshape(C), gk)
 
 
 def solution(mesh):

time: 63.8 us -> 64 us (level)
  other arithmetic: 2.73 us -> 0 us
  Pallas kernels: 57.8 us -> 59.5 us
  local copies, waits for them, and re-layouts: 2.45 us -> 3.53 us
    reshape x2 -> x0, other arithmetic: 2.73 us -> none  [the longest x1 1.87 us: per_device(): g1.astype(F32).reshape(shape)]
    pallas_call x0 -> x1, Pallas kernels: none -> 1.12 us  [per_device(): pl.pallas_call(functools.partial(closing, NX), out_shape=(jax.ShapeDtypeS...]
    unnamed x14 -> x8, local copies, waits for them, and re-layouts: 2.45 us -> 3.53 us
where the time goes in v2:
time: 64 us; the launch traced here: 63.7 us
  Pallas kernels  59.5 us (93%)
  local copies, waits for them, and re-layouts  3.53 us (6%)
  between operations  0.65 us (1%)
    pallas_call x1, Pallas kernels, per_device(): pl.pallas_call(functools.partial(kernel, GX, GY, L, WC, C, CH1, CH2), out...  58.4 us
    unnamed x8, local copies, waits for them, and re-layouts  3.53 us

profile of v2, /device:TPU:1, one launch (start us, length us, event | category | flops | bytes accessed | tf_op | source)
XLA Modules:
  0.0 63.7 jit_solution(12819651280986978318)
XLA Ops:
  0.6 58.4 %shard_map.118 = (bf16[4,128,128]{2,1,0:T(8,128)(2,1)}, bf16[1152,128]{1,0:T(8,128)(2,1)}, bf16[1152,128]{1,0:T(8,128)(2,1)}, bf16[48,128]{1,0:T(8,128)(2,1)}) custom-call(bf16[4,128,128]{2,1,0:T(8,128)(2,1)} %lat_in.1, bf16[32,128]{1,0:T(8,128)(2,1)} %k_in.1, bf16[1152,128]{1,0:T(8,128)(2,1)} %bitcast.10, f32[1,128]{1,0:T(1,128)} %bitcast.12, ...), custom_call_target="tpu_custom_call" | custom-call | flops 2831155200 | bytes 1179648 | tf_op jit(solution)/shard_map/pallas_call | solution.py:497
  59.0 0.0 copy-start
  59.0 1.0 %copy-done = bf16[1152,128]{1,0:T(8,128)(2,1)S(1)} copy-done((bf16[1152,128]{1,0:T(8,128)(2,1)S(1)}, bf16[1152,128]{1,0:T(8,128)(2,1)}, u32[]{:S(2)}) %copy-start) | copy-done | bytes 294936
  60.0 0.0 copy-start.1
  60.0 1.0 %copy-done.1 = bf16[1152,128]{1,0:T(8,128)(2,1)S(1)} copy-done((bf16[1152,128]{1,0:T(8,128)(2,1)S(1)}, bf16[1152,128]{1,0:T(8,128)(2,1)}, u32[]{:S(2)}) %copy-start.1) | copy-done | bytes 294936
  61.0 0.0 copy-start.2
  61.0 0.9 %copy-done.2 = bf16[4,128,128]{2,1,0:T(8,128)(2,1)S(1)} copy-done((bf16[4,128,128]{2,1,0:T(8,128)(2,1)S(1)}, bf16[4,128,128]{2,1,0:T(8,128)(2,1)}, u32[]{:S(2)}) %copy-start.2) | copy-done | bytes 131096
  61.9 0.0 copy-start.3
  61.9 0.7 %copy-done.3 = bf16[48,128]{1,0:T(8,128)(2,1)S(1)} copy-done((bf16[48,128]{1,0:T(8,128)(2,1)S(1)}, bf16[48,128]{1,0:T(8,128)(2,1)}, u32[]{:S(2)}) %copy-start.3) | copy-done | bytes 12312
  62.6 1.1 %shard_map.119 = (bf16[4,128,128]{2,1,0:T(8,128)(2,1)}, f32[1152,128]{1,0:T(8,128)}, f32[1,128]{1,0:T(1,128)}, f32[1152,128]{1,0:T(8,128)}, f32[1,128]{1,0:T(1,128)}, /*index=5*/f32[32,128]{1,0:T(8,128)}) custom-call(bf16[4,128,128]{2,1,0:T(8,128)(2,1)S(1)} %copy-done.2, bf16[1152,128]{1,0:T(8,128)(2,1)S(1)} %copy-done, bf16[1152,128]{1,0:T(8,128)(2,1)S(1)} %copy-done.1, ...), custom_call_target="tpu_custom_call" | custom-call | tf_op jit(solution)/shard_map/pallas_call | solution.py:518
Async XLA Ops:
  59.0 1.0 %copy-start = (bf16[1152,128]{1,0:T(8,128)(2,1)S(1)}, bf16[1152,128]{1,0:T(8,128)(2,1)}, u32[]{:S(2)}) copy-start(bf16[1152,128]{1,0:T(8,128)(2,1)} %get-tuple-element.17.o2) | copy-start | bytes 884740
  60.0 1.0 %copy-start.1 = (bf16[1152,128]{1,0:T(8,128)(2,1)S(1)}, bf16[1152,128]{1,0:T(8,128)(2,1)}, u32[]{:S(2)}) copy-start(bf16[1152,128]{1,0:T(8,128)(2,1)} %get-tuple-element.18.o1) | copy-start | bytes 884740
  61.0 0.9 %copy-start.2 = (bf16[4,128,128]{2,1,0:T(8,128)(2,1)S(1)}, bf16[4,128,128]{2,1,0:T(8,128)(2,1)}, u32[]{:S(2)}) copy-start(bf16[4,128,128]{2,1,0:T(8,128)(2,1)} %get-tuple-element.16.pred) | copy-start | bytes 393220
  61.9 0.7 %copy-start.3 = (bf16[48,128]{1,0:T(8,128)(2,1)S(1)}, bf16[48,128]{1,0:T(8,128)(2,1)}, u32[]{:S(2)}) copy-start(bf16[48,128]{1,0:T(8,128)(2,1)} %get-tuple-element.19.rest) | copy-start | bytes 36868
